TPU v7x, 512 devices: a whole 4x8x8 slice. The times are simulated.
512 devices in a mesh: mem: 64 (over x, y, core), patch: 8 (over z).
Axes of the slice: x: 4, y: 8, z: 8, core: 2. Of those that a mesh axis runs over, the one named last changes fastest.
Arguments:
- state: bfloat16 [3, 1024, 131072], P(None, 'mem', 'patch'), may hold values from -6 to 6
- obs_noise: bfloat16 [1024, 131072], P('mem', 'patch'), may hold values from -6 to 6
- obs_values: float32 [8, 16384], P('patch', 'mem'), may hold values from -6 to 6
- obs_weights: bfloat16 [8, 128, 128, 128], P('patch', 'mem'), may hold values from -1 to 1
- tapers: float32 [8, 128, 128], replicated, may hold values from 0.2 to 1
- pair_source: int32 [8, 128, 4], P('patch', 'mem'), may hold values from 0 to 127, as said below
- pair_taper: int32 [8, 128, 4], P('patch', 'mem'), may hold values from 0 to 7
Outputs:
- analysis: bfloat16 [3, 1024, 131072], P(None, 'mem', 'patch')
Inputs may be any that keep to these rules, and one draw needn't show every extreme that they name: `pair_source`: each listed source lies in the same patch within 2 blocks of its target block; positions beyond the patch's ends are moved to its first or last block.
All inputs are finite; a program needn't handle non-finite values.
Results may differ from a plain program's by a relative error of at most 0.0058.
Values may be sent and summed in bfloat16 or wider, within the bound.
No kernel may reach another device: no remote copies, remote signals or barrier semaphores. Data moves between devices by JAX's collectives and lax.ppermute only.
A program may use at most 64 MiB of HBM per device.

v0:
```python
import jax
import jax.numpy as jnp
from jax import lax
from jax.sharding import PartitionSpec as P

MEMBERS = 1024
VARIABLES = 3
BLOCK_CELLS = 128
RADIUS = 2
PAIRS = 4
BLOCKS_DEV = 2


def padded(cells, sides, width):
    for axis, dim in sides:
        count = lax.axis_size(axis)
        ends = count - 1
        head = lax.slice_in_dim(cells, 0, width, axis=dim)
        tail = lax.slice_in_dim(cells, cells.shape[dim] - width, cells.shape[dim], axis=dim)
        cells = jnp.concatenate(
            [
                lax.ppermute(tail, axis, [(i, (i + 1) % count) for i in range(ends)]),
                cells,
                lax.ppermute(head, axis, [((i + 1) % count, i) for i in range(ends)]),
            ],
            axis=dim,
        )
    return cells


def centered(values):
    wide = values.astype(jnp.float32)
    return (wide - jnp.mean(wide, axis=-2, keepdims=True)).astype(jnp.bfloat16)


def on_device(state, obs_noise, obs_values, obs_weights, tapers, pair_source, pair_taper):
    columns = lax.all_to_all(state, "mem", split_axis=2, concat_axis=1, tiled=True)
    noise_cols = lax.all_to_all(obs_noise, "mem", split_axis=1, concat_axis=0, tiled=True)
    observed = columns[0]
    members = observed.shape[0]
    owned = observed.shape[1]
    anom_first = centered(observed)
    innovation = (
        obs_values[0][None, :] + noise_cols.astype(jnp.float32) - observed.astype(jnp.float32)
    ).astype(jnp.bfloat16)
    weighted = jnp.einsum(
        "nkd,kcd->nkc",
        innovation.reshape(members, BLOCKS_DEV, BLOCK_CELLS),
        obs_weights[0],
        preferred_element_type=jnp.float32,
    )
    weighted = weighted.astype(jnp.bfloat16).reshape(members, owned)
    window = padded(jnp.stack([anom_first, weighted]), (("mem", 2),), RADIUS * BLOCK_CELLS)
    anomalies = centered(columns)
    first_block = lax.axis_index("mem") * BLOCKS_DEV
    results = []
    for block in range(BLOCKS_DEV):
        target_anom = anomalies[:, :, block * BLOCK_CELLS : (block + 1) * BLOCK_CELLS]
        slices = []
        taper_tiles = []
        for slot in range(PAIRS):
            offset = (pair_source[0, block, slot] - first_block + RADIUS) * BLOCK_CELLS
            slices.append(lax.dynamic_slice_in_dim(window, offset, BLOCK_CELLS, 2))
            taper_tiles.append(
                lax.dynamic_index_in_dim(tapers, pair_taper[0, block, slot], 0, keepdims=False)
            )
        sources = jnp.concatenate(slices, axis=2)
        taper_row = jnp.concatenate(taper_tiles, axis=1)
        pieces = []
        for variable in range(VARIABLES):
            covariance = lax.dot_general(
                target_anom[variable],
                sources[0],
                (((0,), (0,)), ((), ())),
                preferred_element_type=jnp.float32,
            ) / (MEMBERS - 1)
            localized = (taper_row * covariance).astype(jnp.bfloat16)
            pieces.append(
                lax.dot_general(
                    sources[1],
                    localized,
                    (((1,), (1,)), ((), ())),
                    preferred_element_type=jnp.float32,
                )
            )
        total = jnp.stack(pieces)
        results.append(total)
    increment = jnp.concatenate(results, axis=2)
    updated = (columns.astype(jnp.float32) + increment).astype(jnp.bfloat16)
    return lax.all_to_all(updated, "mem", split_axis=1, concat_axis=2, tiled=True)


def solution(mesh):
    placed = (
        P(None, "mem", "patch"),
        P("mem", "patch"),
        P("patch", "mem"),
        P("patch", "mem", None, None),
        P(),
        P("patch", "mem", None),
        P("patch", "mem", None),
    )
    return jax.shard_map(
        on_device, mesh=mesh, in_specs=placed, out_specs=P(None, "mem", "patch"), check_vma=False
    )
```

profile of v0, /device:TPU:1, one launch (start us, length us, event | category | flops | bytes accessed | tf_op | source)
XLA Modules:
  0.0 259.1 jit_solution(17874046500938926867)
XLA Ops:
  0.0 2.0 copy.42
  2.0 11.6 %all-to-all-start.1 = ((bf16[16,64,256]{2,0,1:T(8,128)(2,1)}), bf16[16,64,256]{2,0,1:T(8,128)(2,1)S(1)}, u32[]{:S(2)}, u32[]{:S(2)}) async-start(bf16[16,64,256]{2,0,1:T(8,128)(2,1)} %bitcast.125), calls=%async_computation.1 | async-start | bytes 1048576 | tf_op jit(solution)/shard_map/all_to_all | solution.py:38
  13.7 15.7 %copy.24 = bf16[3,16,16384]{1,0,2:T(4,128)(2,1)} copy(bf16[3,16,16384]{2,1,0:T(8,128)(2,1)S(1)} %copy-done.9) | data formatting | bytes 3145728 | tf_op args[0]
  29.4 26.2 %reshape.70 = bf16[64,2,6144]{2,1,0:T(2,128)(2,1)} reshape(bf16[16384,3,16]{2,1,0:T(4,128)(2,1)} %bitcast.127) | data formatting | bytes 3145728
  55.6 10.5 %all-to-all-start = ((bf16[64,2,6144]{2,1,0:T(2,128)(2,1)}), bf16[64,2,6144]{2,1,0:T(2,128)(2,1)S(1)}, u32[]{:S(2)}, u32[]{:S(2)}) async-start(bf16[64,2,6144]{2,1,0:T(2,128)(2,1)} %reshape.70), calls=%async_computation | async-start | bytes 3145728 | tf_op jit(solution)/shard_map/all_to_all | solution.py:37
  88.9 1.5 reshape.68
  90.4 15.4 %all-to-all-done = bf16[64,2,6144]{2,1,0:T(2,128)(2,1)S(1)} async-done(((bf16[64,2,6144]{2,1,0:T(2,128)(2,1)}), bf16[64,2,6144]{2,1,0:T(2,128)(2,1)S(1)}, u32[]{:S(2)}, u32[]{:S(2)}) %all-to-all-start) | async-done | bytes 1572896 | tf_op jit(solution)/shard_map/all_to_all | solution.py:37
  105.9 21.0 %reshape.71 = bf16[16384,3,16]{2,1,0:T(4,128)(2,1)} reshape(bf16[64,2,6144]{2,1,0:T(2,128)(2,1)S(1)} %all-to-all-done) | data formatting | bytes 3145728
  126.9 15.3 %copy.36 = bf16[3,16,64,256]{3,2,1,0:T(8,128)(2,1)S(1)} copy(bf16[3,16,64,256]{1,0,3,2:T(4,128)(2,1)} %bitcast.126) | data formatting | bytes 3145728 | tf_op jit(solution)/shard_map/all_to_all | solution.py:37
  143.0 1.5 reshape.69
  144.6 2.1 subtract_convert_fusion.1
  147.8 1.2 copy.31
  149.1 1.2 pad_maximum_fusion.3
  150.4 2.1 collective-permute-start.1
  152.5 3.7 %collective-permute-start = (bf16[2,1024,256]{2,1,0:T(8,128)(2,1)}, bf16[2,1024,256]{2,1,0:T(8,128)(2,1)}, u32[]{:S(2)}, u32[]{:S(2)}) collective-permute-start(bf16[2,1024,256]{2,1,0:T(8,128)(2,1)} %pad_maximum_fusion.3), channel_id=1, source_target_pairs={{0,8},{8,16},{16,24},{24,32},{32,40},{40,48},{48,56},{56,64},{64,7... | collective-permute-start | bytes 3145736 | tf_op jit(solution)/shard_map/ppermute | solution.py:22
  156.6 1.8 copy.26
  158.4 2.3 copy.32
  160.7 1.7 convert_reduce_fusion
  162.5 1.4 subtract_convert_fusion
  163.9 2.9 %collective-permute-done.1 = bf16[2,1024,256]{2,1,0:T(8,128)(2,1)} collective-permute-done((bf16[2,1024,256]{2,1,0:T(8,128)(2,1)}, bf16[2,1024,256]{2,1,0:T(8,128)(2,1)}, u32[]{:S(2)}, u32[]{:S(2)}) %collective-permute-start.1) | collective-permute-done | bytes 1048608 | tf_op jit(solution)/shard_map/ppermute | solution.py:24
  168.0 1.6 pad_maximum_fusion
  170.6 1.6 pad_maximum_fusion.1
  172.2 3.9 %convolution_bitcast_fusion = f32[1,1024,128]{1,2,0:T(8,128)} fusion(bf16[2,1024,512]{2,1,0:T(8,128)(2,1)} %get-tuple-element.38, bf16[3,1024,256]{2,1,0:T(8,128)(2,1)} %subtract_convert_fusion, f32[128,128]{1,0:T(8,128)S(1)} %copy-done.12, f32[128,128]{1,0:T(8,128)S(1)} %copy-done.13, f32[128,128]{1,0:T(8,128)S(1)} %get-tuple-element.14, ...), kind=kOutput, calls=%fused_computation.7 | convolution fusion | flops 268828672 | bytes 3145728 | tf_op jit(solution)/shard_map/dot_general | solution.py:79
  176.1 3.2 %convolution_bitcast_fusion.1 = f32[1,1024,128]{1,2,0:T(8,128)} fusion(bf16[2,1024,512]{2,1,0:T(8,128)(2,1)} %get-tuple-element.38, bf16[3,1024,256]{2,1,0:T(8,128)(2,1)} %subtract_convert_fusion, f32[128,128]{1,0:T(8,128)S(1)} %copy-done.12, f32[128,128]{1,0:T(8,128)S(1)} %copy-done.13, f32[128,128]{1,0:T(8,128)S(1)} %get-tuple-element.14, ...), kind=kOutput, calls=%fused_computation.8 | convolution fusion | flops 268828672 | bytes 3145728 | tf_op jit(solution)/shard_map/dot_general | solution.py:79
  179.3 3.2 %convolution_bitcast_fusion.2 = f32[1,1024,128]{1,2,0:T(8,128)} fusion(bf16[2,1024,512]{2,1,0:T(8,128)(2,1)} %get-tuple-element.38, bf16[3,1024,256]{2,1,0:T(8,128)(2,1)} %subtract_convert_fusion, f32[128,128]{1,0:T(8,128)S(1)} %copy-done.12, f32[128,128]{1,0:T(8,128)S(1)} %copy-done.13, f32[128,128]{1,0:T(8,128)S(1)} %get-tuple-element.14, ...), kind=kOutput, calls=%fused_computation.9 | convolution fusion | flops 268828672 | bytes 3145728 | tf_op jit(solution)/shard_map/dot_general | solution.py:79
  182.5 2.5 convolution_bitcast_fusion.3
  184.9 2.5 convolution_bitcast_fusion.4
  187.4 3.3 %convolution_bitcast_fusion.5 = f32[1,1024,128]{1,2,0:T(8,128)} fusion(bf16[2,1024,512]{2,1,0:T(8,128)(2,1)} %copy-done.8, bf16[3,1024,256]{2,1,0:T(8,128)(2,1)} %subtract_convert_fusion, f32[128,128]{1,0:T(8,128)S(1)} %get-tuple-element.16, f32[128,128]{1,0:T(8,128)S(1)} %get-tuple-element.17, f32[128,128]{1,0:T(8,128)S(1)} %get-tuple-element.18, ...), kind=kOutput, calls=%fused_computation.12 | convolution fusion | flops 268828672 | bytes 3145728 | tf_op jit(solution)/shard_map/dot_general | solution.py:79
  190.7 3.5 %fusion = bf16[3,1024,256]{1,2,0:T(8,128)(2,1)} fusion(f32[3,1024,256]{1,2,0:T(8,128)S(1)} %copy-done.3, f32[1,1024,128]{1,2,0:T(8,128)} %convolution_bitcast_fusion, f32[1,1024,128]{1,2,0:T(8,128)} %convolution_bitcast_fusion.1, f32[1,1024,128]{1,2,0:T(8,128)} %convolution_bitcast_fusion.2, f32[1,1024,128]{1,2,0:T(8,128)} %convolution_bitcast_fusion.3, ...), kind=kLoop, calls=%fused_computation.2 | loop fusion | flops 5505024 | bytes 7864320 | tf_op jit(solution)/shard_map/convert_element_type | solution.py:89
  194.2 2.9 %copy.33 = bf16[3,1024,256]{2,0,1:T(4,128)(2,1)S(1)} copy(bf16[3,1024,256]{1,2,0:T(8,128)(2,1)} %fusion) | data formatting | bytes 3145728 | tf_op jit(solution)/shard_map/convert_element_type | solution.py:89
  197.1 60.5 %all_to_all.46 = bf16[3,1024,256]{2,0,1:T(4,128)(2,1)S(1)} all-to-all(bf16[3,1024,256]{2,0,1:T(4,128)(2,1)S(1)} %copy.33), channel_id=1, replica_groups=mesh['mem'=64,'patch'=8] {'mem'}, dimensions={1} | all-to-all | bytes 3145728 | tf_op jit(solution)/shard_map/all_to_all | solution.py:90
  257.8 1.2 copy.38
  (50 shorter events, 7.1 us)
Async XLA Ops:
  0.0 146.6 %copy-start = (bf16[1,2,128,128]{3,2,1,0:T(8,128)(2,1)S(1)}, bf16[1,2,128,128]{3,2,1,0:T(8,128)(2,1)}, u32[]{:S(2)}) copy-start(bf16[1,2,128,128]{3,2,1,0:T(8,128)(2,1)} %param.10) | copy-start | bytes 196612
  0.0 13.6 %copy-start.9 = (bf16[3,16,16384]{2,1,0:T(8,128)(2,1)S(1)}, bf16[3,16,16384]{2,1,0:T(8,128)(2,1)}, u32[]{:S(2)}) copy-start(bf16[3,16,16384]{2,1,0:T(8,128)(2,1)} %param.7) | copy-start | bytes 4718596
  2.0 53.6 %all-to-all-start.1 = ((bf16[16,64,256]{2,0,1:T(8,128)(2,1)}), bf16[16,64,256]{2,0,1:T(8,128)(2,1)S(1)}, u32[]{:S(2)}, u32[]{:S(2)}) async-start(bf16[16,64,256]{2,0,1:T(8,128)(2,1)} %bitcast.125), calls=%async_computation.1 | async-start | bytes 1048576 | tf_op jit(solution)/shard_map/all_to_all | solution.py:38
  55.6 10.5 %copy-start.14 = (s32[1,2,4]{2,1,0:T(2,128)S(1)}, s32[1,2,4]{2,1,0:T(2,128)}, u32[]{:S(2)}) copy-start(s32[1,2,4]{2,1,0:T(2,128)} %param.12) | copy-start | bytes 100
  55.6 16.4 %copy-start.15 = (s32[1,2,4]{2,1,0:T(2,128)S(1)}, s32[1,2,4]{2,1,0:T(2,128)}, u32[]{:S(2)}) copy-start(s32[1,2,4]{2,1,0:T(2,128)} %param.13) | copy-start | bytes 100
  55.6 32.5 %copy-start.10 = (f32[8,128,128]{2,1,0:T(8,128)S(1)}, f32[8,128,128]{2,1,0:T(8,128)}, u32[]{:S(2)}) copy-start(f32[8,128,128]{2,1,0:T(8,128)} %param.11) | copy-start | bytes 1572868
  55.6 50.3 %all-to-all-start = ((bf16[64,2,6144]{2,1,0:T(2,128)(2,1)}), bf16[64,2,6144]{2,1,0:T(2,128)(2,1)S(1)}, u32[]{:S(2)}, u32[]{:S(2)}) async-start(bf16[64,2,6144]{2,1,0:T(2,128)(2,1)} %reshape.70), calls=%async_computation | async-start | bytes 3145728 | tf_op jit(solution)/shard_map/all_to_all | solution.py:37
  142.1 14.0 %copy-start.2 = (bf16[3,16,64,256]{3,2,1,0:T(8,128)(2,1)}, bf16[3,16,64,256]{3,2,1,0:T(8,128)(2,1)S(1)}, u32[]{:S(2)}) copy-start(bf16[3,16,64,256]{3,2,1,0:T(8,128)(2,1)S(1)} %copy.36) | copy-start | bytes 4718596
  142.4 2.1 copy-start.16
  149.0 7.1 %copy-start.4 = (bf16[1,1024,256]{2,1,0:T(8,128)(2,1)}, bf16[1,1024,256]{2,1,0:T(8,128)(2,1)S(1)}, u32[]{:S(2)}) copy-start(bf16[1,1024,256]{2,1,0:T(8,128)(2,1)S(1)} %copy.31) | copy-start | bytes 1572868
  149.1 3.3 %copy-start.6 = (bf16[1,1024,256]{2,1,0:T(8,128)(2,1)}, bf16[1,1024,256]{2,1,0:T(8,128)(2,1)S(1)}, u32[]{:S(2)}) copy-start(bf16[1,1024,256]{2,1,0:T(8,128)(2,1)S(1)} %fusion.13) | copy-start | bytes 1572868
  150.4 16.4 %collective-permute-start.1 = (bf16[2,1024,256]{2,1,0:T(8,128)(2,1)}, bf16[2,1024,256]{2,1,0:T(8,128)(2,1)}, u32[]{:S(2)}, u32[]{:S(2)}) collective-permute-start(bf16[2,1024,256]{2,1,0:T(8,128)(2,1)} %pad_maximum_fusion.3), channel_id=1, source_target_pairs={{8,0},{16,8},{24,16},{32,24},{40,32},{48,40},{56,48},{64,56},{72,6... | collective-permute-start | bytes 3145736 | tf_op jit(solution)/shard_map/ppermute | solution.py:24
  152.5 15.5 %collective-permute-start = (bf16[2,1024,256]{2,1,0:T(8,128)(2,1)}, bf16[2,1024,256]{2,1,0:T(8,128)(2,1)}, u32[]{:S(2)}, u32[]{:S(2)}) collective-permute-start(bf16[2,1024,256]{2,1,0:T(8,128)(2,1)} %pad_maximum_fusion.3), channel_id=1, source_target_pairs={{0,8},{8,16},{16,24},{24,32},{32,40},{40,48},{48,56},{56,64},{64,7... | collective-permute-start | bytes 3145736 | tf_op jit(solution)/shard_map/ppermute | solution.py:22
  162.4 5.6 %copy-start.5 = (bf16[1,1024,256]{2,1,0:T(8,128)(2,1)S(1)}, bf16[1,1024,256]{2,1,0:T(8,128)(2,1)}, u32[]{:S(2)}) copy-start(bf16[1,1024,256]{2,1,0:T(8,128)(2,1)} %copy-done.4) | copy-start | bytes 1572868
  162.5 5.6 %copy-start.7 = (bf16[1,1024,256]{2,1,0:T(8,128)(2,1)S(1)}, bf16[1,1024,256]{2,1,0:T(8,128)(2,1)}, u32[]{:S(2)}) copy-start(bf16[1,1024,256]{2,1,0:T(8,128)(2,1)} %copy-done.6) | copy-start | bytes 1572868
  170.5 1.6 copy-start.11
  170.6 1.6 copy-start.12
  170.6 1.6 copy-start.13
  172.2 12.8 %copy-start.8 = (bf16[2,1024,512]{2,1,0:T(8,128)(2,1)}, bf16[2,1024,512]{2,1,0:T(8,128)(2,1)S(1)}, u32[]{:S(2)}) copy-start(bf16[2,1024,512]{2,1,0:T(8,128)(2,1)S(1)} %get-tuple-element.37) | copy-start | bytes 6291460
  187.4 3.3 %copy-start.3 = (f32[3,1024,256]{1,2,0:T(8,128)S(1)}, f32[3,1024,256]{1,2,0:T(8,128)}, u32[]{:S(2)}) copy-start(f32[3,1024,256]{1,2,0:T(8,128)} %copy.32) | copy-start | bytes 9437188
  257.6 1.5 copy-start.1
where the time goes:
time: 261 us; the launch traced here: 259 us
  local copies, waits for them, and re-layouts  96.7 us (37%)
  blocking collectives  60.5 us (23%)
  starting transfers between devices  27.8 us (11%)
  between operations  20.9 us (8%)
  matrix products  19.6 us (8%)
  waiting for transfers between devices  19.5 us (7%)
  other arithmetic  14 us (5%)
    unnamed x37, local copies, waits for them, and re-layouts  63 us
    all_to_all x1, blocking collectives, on_device(): lax.all_to_all(updated, 'mem', split_axis=1, concat_axis=2, tiled=True)  60.5 us
    dot_general x6, matrix products, on_device(): lax.dot_general(sources[1], localized, (((1,), (1,)), ((), ())), preferre...  18.5 us
    all_to_all x1, waiting for transfers between devices, on_device(): lax.all_to_all(state, 'mem', split_axis=2, concat_axis=1, tiled=True)  15.4 us
    all_to_all x1, local copies, waits for them, and re-layouts, on_device(): lax.all_to_all(state, 'mem', split_axis=2, concat_axis=1, tiled=True)  15.3 us
    all_to_all x1, starting transfers between devices, on_device(): lax.all_to_all(obs_noise, 'mem', split_axis=1, concat_axis=0, tiled=True)  11.6 us
    all_to_all x1, starting transfers between devices, on_device(): lax.all_to_all(state, 'mem', split_axis=2, concat_axis=1, tiled=True)  10.5 us
    convert_element_type x3, local copies, waits for them, and re-layouts, on_device(): updated = (columns.astype(jnp.float32) + increment).astype(jnp.bfloat16)  7.09 us
  transfers between devices with their start and end apart: 4, of which 3 were waited for; matrix products, arithmetic and copies ran while one was open for 21% of the time, Pallas kernels for 0%

commit v1 on v0

--- a/solution.py
+++ b/solution.py
@@ -9,6 +9,19 @@
 RADIUS = 2
 PAIRS = 4
 BLOCKS_DEV = 2
+
+
+def _feed_knots(target, mesh_dim, array_axis, join_dim):
+    passed = jnp.concatenate(
+        jax.lax.all_to_all(
+            jnp.stack(jnp.split(target, jax.lax.axis_size(mesh_dim), array_axis), axis=0),
+            mesh_dim,
+            0,
+            0,
+        ),
+        join_dim,
+    )
+    return passed
 
 
 def padded(cells, sides, width):
@@ -34,7 +47,7 @@
 
 
 def on_device(state, obs_noise, obs_values, obs_weights, tapers, pair_source, pair_taper):
-    columns = lax.all_to_all(state, "mem", split_axis=2, concat_axis=1, tiled=True)
+    columns = _feed_knots(state, "mem", 2, 1)
     noise_cols = lax.all_to_all(obs_noise, "mem", split_axis=1, concat_axis=0, tiled=True)
     observed = columns[0]
     members = observed.shape[0]

time: 261 us -> 241 us (0.923)
  local copies, waits for them, and re-layouts: 96.7 us -> 59.3 us
  waiting for transfers between devices: 19.5 us -> 38.1 us
  other arithmetic: 14 us -> 17.6 us
  blocking collectives: 60.5 us -> 57.1 us
    unnamed x37 -> x93, local copies, waits for them, and re-layouts: 63 us -> 39.5 us
    all_to_all x1, waiting for transfers between devices: 15.4 us -> 38.1 us  [_feed_knots(): jax.lax.all_to_all(jnp.stack(jnp.split(target, jax.lax.axis_size(mesh_dim...]
    all_to_all x1 -> x0, local copies, waits for them, and re-layouts: 15.3 us -> none  [on_device(): lax.all_to_all(state, 'mem', split_axis=2, concat_axis=1, tiled=True)]
    all_to_all x1, blocking collectives: 60.5 us -> 57.1 us  [on_device(): lax.all_to_all(updated, 'mem', split_axis=1, concat_axis=2, tiled=True)]
    convert_element_type x2, local copies, waits for them, and re-layouts: 2.13 us -> 5.28 us  [centered(): wide = values.astype(jnp.float32)]
    ppermute x1, waiting for transfers between devices: 2.92 us -> 0.01 us  [padded(): lax.ppermute(head, axis, [((i + 1) % count, i) for i in range(ends)])]
    convert_element_type x3 -> x2, local copies, waits for them, and re-layouts: 7.09 us -> 5.26 us  [on_device(): updated = (columns.astype(jnp.float32) + increment).astype(jnp.bfloat16)]
  transfers between devices with their start and end apart: 4 -> 4, of which waited for: 3 -> 1; matrix products, arithmetic and copies ran while one was open for 21% -> 21% of each run, Pallas kernels for 0% -> 0%
where the time goes in v1:
time: 241 us; the launch traced here: 240 us
  local copies, waits for them, and re-layouts  59.3 us (25%)
  blocking collectives  57.1 us (24%)
  waiting for transfers between devices  38.1 us (16%)
  starting transfers between devices  27.8 us (12%)
  between operations  20.7 us (9%)
  matrix products  18.9 us (8%)
  other arithmetic  17.6 us (7%)
    all_to_all x1, blocking collectives, on_device(): lax.all_to_all(updated, 'mem', split_axis=1, concat_axis=2, tiled=True)  57.1 us
    unnamed x93, local copies, waits for them, and re-layouts  39.5 us
    all_to_all x1, waiting for transfers between devices, _feed_knots(): jax.lax.all_to_all(jnp.stack(jnp.split(target, jax.lax.axis_size(mesh_dim...  38.1 us
    dot_general x6, matrix products, on_device(): lax.dot_general(sources[1], localized, (((1,), (1,)), ((), ())), preferre...  18.6 us
    all_to_all x1, starting transfers between devices, on_device(): lax.all_to_all(obs_noise, 'mem', split_axis=1, concat_axis=0, tiled=True)  11.6 us
    all_to_all x1, starting transfers between devices, _feed_knots(): jax.lax.all_to_all(jnp.stack(jnp.split(target, jax.lax.axis_size(mesh_dim...  10.5 us
    convert_element_type x2, local copies, waits for them, and re-layouts, centered(): wide = values.astype(jnp.float32)  5.28 us
    convert_element_type x2, local copies, waits for them, and re-layouts, on_device(): updated = (columns.astype(jnp.float32) + increment).astype(jnp.bfloat16)  5.26 us
  transfers between devices with their start and end apart: 4, of which 1 were waited for; matrix products, arithmetic and copies ran while one was open for 21% of the time, Pallas kernels for 0%

profile of v1, /device:TPU:1, one launch (start us, length us, event | category | flops | bytes accessed | tf_op | source)
XLA Modules:
  0.0 239.5 jit_solution(1340998057227788498)
XLA Ops:
  0.0 2.0 copy.41
  2.0 11.6 %all-to-all-start.1 = ((bf16[16,64,256]{2,0,1:T(8,128)(2,1)}), bf16[16,64,256]{2,0,1:T(8,128)(2,1)S(1)}, u32[]{:S(2)}, u32[]{:S(2)}) async-start(bf16[16,64,256]{2,0,1:T(8,128)(2,1)} %bitcast.250), calls=%async_computation.1 | async-start | bytes 1048576 | tf_op jit(solution)/shard_map/all_to_all | solution.py:51
  52.8 10.5 %all-to-all-start = ((bf16[64,3,16,256]{3,2,1,0:T(8,128)(2,1)}), bf16[64,3,16,256]{3,2,1,0:T(8,128)(2,1)}, u32[]{:S(2)}, u32[]{:S(2)}) async-start(bf16[64,3,16,256]{3,2,1,0:T(8,128)(2,1)} %constant_dynamic-update-slice_fusion), calls=%async_computation | async-start | bytes 3145728 | tf_op jit(solution)/shard_map/all_to_all | solution.py:16
  63.4 1.5 reshape.73
  64.9 38.1 %all-to-all-done = bf16[64,3,16,256]{3,2,1,0:T(8,128)(2,1)} async-done(((bf16[64,3,16,256]{3,2,1,0:T(8,128)(2,1)}), bf16[64,3,16,256]{3,2,1,0:T(8,128)(2,1)}, u32[]{:S(2)}, u32[]{:S(2)}) %all-to-all-start) | async-done | bytes 1572896 | tf_op jit(solution)/shard_map/all_to_all | solution.py:16
  103.0 1.9 copy_bitcast_fusion
  105.1 1.1 slice_convert_fusion
  106.2 2.7 %reshape.74 = f32[1024,2,128]{2,1,0:T(2,128)} reshape(f32[1,64,16,256]{3,2,1,0:T(8,128)} %slice_convert_fusion) | data formatting | bytes 2097152 | tf_op jit(solution)/shard_map/convert_element_type | solution.py:45
  108.9 2.5 %copy.24 = f32[1,1024,256]{1,2,0:T(8,128)} copy(f32[1,1024,256]{2,1,0:T(8,128)} %bitcast.252) | data formatting | bytes 2097152 | tf_op jit(solution)/shard_map/convert_element_type | solution.py:45
  111.5 1.4 subtract_convert_fusion.2
  113.0 1.9 subtract_convert_fusion.1
  115.3 0.8 copy-done.2
  116.1 1.1 pad_maximum_fusion.3
  117.2 2.1 collective-permute-start.1
  119.2 3.7 %collective-permute-start = (bf16[2,1024,256]{1,2,0:T(8,128)(2,1)}, bf16[2,1024,256]{1,2,0:T(8,128)(2,1)}, u32[]{:S(2)}, u32[]{:S(2)}) collective-permute-start(bf16[2,1024,256]{1,2,0:T(8,128)(2,1)} %pad_maximum_fusion.3), channel_id=1, source_target_pairs={{0,8},{8,16},{16,24},{24,32},{32,40},{40,48},{48,56},{56,64},{64,7... | collective-permute-start | bytes 3145736 | tf_op jit(solution)/shard_map/ppermute | solution.py:35
  122.9 0.7 fusion.36
  144.7 1.8 dynamic-slice_bitcast_fusion.7
  146.5 2.3 copy.27
  148.8 1.7 convert_reduce_fusion
  150.5 1.4 subtract_convert_fusion
  151.9 1.8 pad_maximum_fusion
  154.4 1.6 pad_maximum_fusion.1
  155.9 3.9 %convolution_bitcast_fusion = f32[1,1024,128]{1,2,0:T(8,128)} fusion(bf16[2,1024,512]{1,2,0:T(8,128)(2,1)} %get-tuple-element.40, bf16[3,1024,256]{2,1,0:T(8,128)(2,1)} %subtract_convert_fusion, f32[128,128]{1,0:T(8,128)S(1)} %copy-done.10, f32[128,128]{1,0:T(8,128)S(1)} %copy-done.11, f32[128,128]{1,0:T(8,128)S(1)} %get-tuple-element.16, ...), kind=kOutput, calls=%fused_computation.8 | convolution fusion | flops 268828672 | bytes 3145728 | tf_op jit(solution)/shard_map/dot_general | solution.py:92
  159.9 3.2 %convolution_bitcast_fusion.1 = f32[1,1024,128]{1,2,0:T(8,128)} fusion(bf16[2,1024,512]{1,2,0:T(8,128)(2,1)} %get-tuple-element.40, bf16[3,1024,256]{2,1,0:T(8,128)(2,1)} %subtract_convert_fusion, f32[128,128]{1,0:T(8,128)S(1)} %copy-done.10, f32[128,128]{1,0:T(8,128)S(1)} %copy-done.11, f32[128,128]{1,0:T(8,128)S(1)} %get-tuple-element.16, ...), kind=kOutput, calls=%fused_computation.9 | convolution fusion | flops 268828672 | bytes 3145728 | tf_op jit(solution)/shard_map/dot_general | solution.py:92
  163.1 3.2 %convolution_bitcast_fusion.2 = f32[1,1024,128]{1,2,0:T(8,128)} fusion(bf16[2,1024,512]{1,2,0:T(8,128)(2,1)} %get-tuple-element.40, bf16[3,1024,256]{2,1,0:T(8,128)(2,1)} %subtract_convert_fusion, f32[128,128]{1,0:T(8,128)S(1)} %copy-done.10, f32[128,128]{1,0:T(8,128)S(1)} %copy-done.11, f32[128,128]{1,0:T(8,128)S(1)} %get-tuple-element.16, ...), kind=kOutput, calls=%fused_computation.10 | convolution fusion | flops 268828672 | bytes 3145728 | tf_op jit(solution)/shard_map/dot_general | solution.py:92
  166.3 2.5 %convolution_bitcast_fusion.3 = f32[1,1024,128]{1,2,0:T(8,128)} fusion(bf16[2,1024,512]{1,2,0:T(8,128)(2,1)S(1)} %get-tuple-element.39, bf16[3,1024,256]{2,1,0:T(8,128)(2,1)} %subtract_convert_fusion, f32[128,128]{1,0:T(8,128)S(1)} %get-tuple-element.18, f32[128,128]{1,0:T(8,128)S(1)} %get-tuple-element.19, f32[128,128]{1,0:T(8,128)S(1)} %get-tuple-element.20, ...), kind=kOutput, calls=%fused_computation.11 | convolution fusion | flops 268828672 | bytes 3145728 | tf_op jit(solution)/shard_map/dot_general | solution.py:92
  168.8 2.5 %convolution_bitcast_fusion.4 = f32[1,1024,128]{1,2,0:T(8,128)} fusion(bf16[2,1024,512]{1,2,0:T(8,128)(2,1)S(1)} %get-tuple-element.39, bf16[3,1024,256]{2,1,0:T(8,128)(2,1)} %subtract_convert_fusion, f32[128,128]{1,0:T(8,128)S(1)} %get-tuple-element.18, f32[128,128]{1,0:T(8,128)S(1)} %get-tuple-element.19, f32[128,128]{1,0:T(8,128)S(1)} %get-tuple-element.20, ...), kind=kOutput, calls=%fused_computation.12 | convolution fusion | flops 268828672 | bytes 3145728 | tf_op jit(solution)/shard_map/dot_general | solution.py:92
  171.3 3.3 %convolution_bitcast_fusion.5 = f32[1,1024,128]{1,2,0:T(8,128)} fusion(bf16[2,1024,512]{1,2,0:T(8,128)(2,1)} %copy-done.7, bf16[3,1024,256]{2,1,0:T(8,128)(2,1)} %subtract_convert_fusion, f32[128,128]{1,0:T(8,128)S(1)} %get-tuple-element.18, f32[128,128]{1,0:T(8,128)S(1)} %get-tuple-element.19, f32[128,128]{1,0:T(8,128)S(1)} %get-tuple-element.20, ...), kind=kOutput, calls=%fused_computation.13 | convolution fusion | flops 268828672 | bytes 3145728 | tf_op jit(solution)/shard_map/dot_general | solution.py:92
  174.6 3.5 %fusion = bf16[3,1024,256]{1,2,0:T(8,128)(2,1)} fusion(f32[3,1024,256]{1,2,0:T(8,128)S(1)} %copy-done.1, f32[1,1024,128]{1,2,0:T(8,128)} %convolution_bitcast_fusion, f32[1,1024,128]{1,2,0:T(8,128)} %convolution_bitcast_fusion.1, f32[1,1024,128]{1,2,0:T(8,128)} %convolution_bitcast_fusion.2, f32[1,1024,128]{1,2,0:T(8,128)} %convolution_bitcast_fusion.3, ...), kind=kLoop, calls=%fused_computation.2 | loop fusion | flops 5505024 | bytes 7864320 | tf_op jit(solution)/shard_map/convert_element_type | solution.py:102
  178.0 2.9 %copy.28 = bf16[3,1024,256]{2,0,1:T(4,128)(2,1)S(1)} copy(bf16[3,1024,256]{1,2,0:T(8,128)(2,1)} %fusion) | data formatting | bytes 3145728 | tf_op jit(solution)/shard_map/convert_element_type | solution.py:102
  181.0 57.1 %all_to_all.36 = bf16[3,1024,256]{2,0,1:T(4,128)(2,1)S(1)} all-to-all(bf16[3,1024,256]{2,0,1:T(4,128)(2,1)S(1)} %copy.28), channel_id=1, replica_groups=mesh['mem'=64,'patch'=8] {'mem'}, dimensions={1} | all-to-all | bytes 3145728 | tf_op jit(solution)/shard_map/all_to_all | solution.py:103
  238.3 1.2 copy.32
  (104 shorter events, 41.4 us)
Async XLA Ops:
  0.0 114.9 %copy-start = (bf16[1,2,128,128]{3,2,1,0:T(8,128)(2,1)S(1)}, bf16[1,2,128,128]{3,2,1,0:T(8,128)(2,1)}, u32[]{:S(2)}) copy-start(bf16[1,2,128,128]{3,2,1,0:T(8,128)(2,1)} %param.10) | copy-start | bytes 196612
  0.0 13.6 %copy-start.8 = (bf16[3,16,16384]{2,1,0:T(8,128)(2,1)S(1)}, bf16[3,16,16384]{2,1,0:T(8,128)(2,1)}, u32[]{:S(2)}) copy-start(bf16[3,16,16384]{2,1,0:T(8,128)(2,1)} %param.7) | copy-start | bytes 4718596
  2.0 50.8 %all-to-all-start.1 = ((bf16[16,64,256]{2,0,1:T(8,128)(2,1)}), bf16[16,64,256]{2,0,1:T(8,128)(2,1)S(1)}, u32[]{:S(2)}, u32[]{:S(2)}) async-start(bf16[16,64,256]{2,0,1:T(8,128)(2,1)} %bitcast.250), calls=%async_computation.1 | async-start | bytes 1048576 | tf_op jit(solution)/shard_map/all_to_all | solution.py:51
  52.8 50.2 %all-to-all-start = ((bf16[64,3,16,256]{3,2,1,0:T(8,128)(2,1)}), bf16[64,3,16,256]{3,2,1,0:T(8,128)(2,1)}, u32[]{:S(2)}, u32[]{:S(2)}) async-start(bf16[64,3,16,256]{3,2,1,0:T(8,128)(2,1)} %constant_dynamic-update-slice_fusion), calls=%async_computation | async-start | bytes 3145728 | tf_op jit(solution)/shard_map/all_to_all | solution.py:16
  108.9 4.0 %copy-start.14 = (f32[1,256]{1,0:T(1,128)S(1)}, f32[1,256]{1,0:T(1,128)}, u32[]{:S(2)}) copy-start(f32[1,256]{1,0:T(1,128)} %param.9) | copy-start | bytes 3076
  111.5 1.5 copy-start.6
  112.9 2.3 copy-start.4
  114.9 8.0 %copy-start.12 = (s32[1,2,4]{2,1,0:T(2,128)S(1)}, s32[1,2,4]{2,1,0:T(2,128)}, u32[]{:S(2)}) copy-start(s32[1,2,4]{2,1,0:T(2,128)} %param.12) | copy-start | bytes 100
  114.9 13.8 %copy-start.13 = (s32[1,2,4]{2,1,0:T(2,128)S(1)}, s32[1,2,4]{2,1,0:T(2,128)}, u32[]{:S(2)}) copy-start(s32[1,2,4]{2,1,0:T(2,128)} %param.13) | copy-start | bytes 100
  115.3 0.9 copy-start.2
  117.2 34.7 %collective-permute-start.1 = (bf16[2,1024,256]{1,2,0:T(8,128)(2,1)}, bf16[2,1024,256]{1,2,0:T(8,128)(2,1)}, u32[]{:S(2)}, u32[]{:S(2)}) collective-permute-start(bf16[2,1024,256]{1,2,0:T(8,128)(2,1)} %pad_maximum_fusion.3), channel_id=1, source_target_pairs={{8,0},{16,8},{24,16},{32,24},{40,32},{48,40},{56,48},{64,56},{72,6... | collective-permute-start | bytes 3145736 | tf_op jit(solution)/shard_map/ppermute | solution.py:37
  119.2 32.7 %collective-permute-start = (bf16[2,1024,256]{1,2,0:T(8,128)(2,1)}, bf16[2,1024,256]{1,2,0:T(8,128)(2,1)}, u32[]{:S(2)}, u32[]{:S(2)}) collective-permute-start(bf16[2,1024,256]{1,2,0:T(8,128)(2,1)} %pad_maximum_fusion.3), channel_id=1, source_target_pairs={{0,8},{8,16},{16,24},{24,32},{32,40},{40,48},{48,56},{56,64},{64,7... | collective-permute-start | bytes 3145736 | tf_op jit(solution)/shard_map/ppermute | solution.py:35
  150.5 1.5 copy-start.3
  150.5 1.5 copy-start.5
  154.3 1.6 copy-start.9
  154.3 1.6 copy-start.10
  154.4 1.6 copy-start.11
  155.9 12.8 %copy-start.7 = (bf16[2,1024,512]{1,2,0:T(8,128)(2,1)}, bf16[2,1024,512]{1,2,0:T(8,128)(2,1)S(1)}, u32[]{:S(2)}) copy-start(bf16[2,1024,512]{1,2,0:T(8,128)(2,1)S(1)} %get-tuple-element.39) | copy-start | bytes 6291460
  171.3 3.3 %copy-start.1 = (f32[3,1024,256]{1,2,0:T(8,128)S(1)}, f32[3,1024,256]{1,2,0:T(8,128)}, u32[]{:S(2)}) copy-start(f32[3,1024,256]{1,2,0:T(8,128)} %copy.27) | copy-start | bytes 9437188
